TPU v7x, 128 devices: a whole 4x4x4 slice. The times are simulated.
128 devices in a mesh: lat: 16 (over z, x), lon: 8 (over y, core).
Axes of the slice: x: 4, y: 4, z: 4, core: 2. Of those that a mesh axis runs over, the one named last changes fastest.
Arguments:
- field: bfloat16 [69, 512, 4096], P(None, 'lat', 'lon'), may hold values from -6 to 6
- stem_weight: bfloat16 [1104, 512], replicated, may hold values from -0.1875 to 0.1875
- stem_bias: float32 [512], replicated, may hold values from -3 to 3
- token_gain: float32 [512], replicated, may hold values from 0.1 to 1.9
- kv_weight: bfloat16 [512, 1024], replicated, may hold values from -0.25 to 0.25
- latents: float32 [512, 512], replicated, may hold values from -6 to 6
- latent_gain: float32 [512], replicated, may hold values from 0.1 to 1.9
- query_weight: bfloat16 [512, 512], replicated, may hold values from -0.25 to 0.25
- head_gain: float32 [8], replicated, may hold values from 2 to 40
- out_weight: bfloat16 [512, 512], replicated, may hold values from -0.25 to 0.25
- out_gain: float32 [512], replicated, may hold values from 0.1 to 1.9
Outputs:
- tokens: bfloat16 [256, 2048, 512], P('lat', 'lon')
- latent_out: float32 [512, 512], replicated
All inputs are finite; a program needn't handle non-finite values.
Results may differ from a plain program's by a relative error of at most 0.015.
The roundings to bfloat16 on the way count: a program that leaves them out, or rounds other values in their place, can miss the bound.
Values may be sent and summed in bfloat16 or wider, within the bound.
A program may use at most 512 MiB of HBM per device.

v0:
```python
import functools

import jax
import jax.numpy as jnp
from jax import lax
from jax.experimental import pallas as pl
from jax.experimental.pallas import tpu as pltpu
from jax.sharding import PartitionSpec as P

HEADS = 8
HD = 64
LAT = 512
D = 512
CHAN = 69
CPAD = 80
ROWS = 32
COLS = 512
TH = 16
TW = 256
TOK = TH * TW
SLAB = 4 * CPAD
NLATD = 16
NLOND = 8
EXT = 80
CH = 1024
MESH = pl.DeviceIdType.MESH
F32 = jnp.float32
BF = jnp.bfloat16
VM = pl.BlockSpec(memory_space=pltpu.VMEM)
SM = pl.BlockSpec(memory_space=pltpu.SMEM)
ANY = pl.BlockSpec(memory_space=pl.ANY)


def remote(src, dst, send, recv, target):
    return pltpu.make_async_remote_copy(
        src_ref=src, dst_ref=dst, send_sem=send, recv_sem=recv, device_id=target, device_id_type=MESH
    )


def prep_kernel(
    field_ref, sw_ref, kvw_ref, latents_ref, lgain_ref, qw_ref,
    sl_ref, wt_ref, wvt_ref, qt_ref,
    g_ref, wf_ref, wp_ref, cols_ref, colr_ref, rowr_ref, send_sem, recv_sem,
):
    lat = lax.axis_index("lat")
    lon = lax.axis_index("lon")
    up, down = lax.rem(lat + NLATD - 1, NLATD), lax.rem(lat + 1, NLATD)
    left, right = lax.rem(lon + NLOND - 1, NLOND), lax.rem(lon + 1, NLOND)
    barrier = pltpu.get_barrier_semaphore()
    around = [(lat, left), (lat, right), (up, lon), (down, lon), (up, left), (up, right), (down, left), (down, right)]
    for target in around:
        pl.semaphore_signal(barrier, inc=1, device_id=target, device_id_type=MESH)

    source = lax.broadcasted_iota(jnp.int32, (256, 256), 0)
    place = lax.broadcasted_iota(jnp.int32, (256, 256), 1)
    wanted = jnp.where(place < 128, 2 * place, 2 * (place - 128) + 1)
    select = (source == wanted).astype(F32).astype(BF)
    for half in range(2):
        block = field_ref[:, :, half * 256:(half + 1) * 256].reshape(CHAN * ROWS, 256)
        both = jnp.dot(block, select, preferred_element_type=F32)
        g_ref[half, 0:CHAN * ROWS, :] = both[:, :128]
        g_ref[2 + half, 0:CHAN * ROWS, :] = both[:, 128:]
    g_ref[:, CHAN * ROWS:CPAD * ROWS, :] = jnp.zeros((4, (CPAD - CHAN) * ROWS, 128), F32)

    lane = lax.broadcasted_iota(jnp.int32, (CPAD, 128), 1)

    def spread(y, carry):
        first, last = carry
        quarter = [g_ref[n, pl.ds(y, CPAD, stride=ROWS), :] for n in range(4)]
        even = jnp.concatenate(quarter[:2], axis=1)
        odd = jnp.concatenate(quarter[2:], axis=1)
        base = pl.multiple_of((y + 1) * SLAB, SLAB)
        sl_ref[pl.ds(base, CPAD), :] = pltpu.roll(odd, 1, 1).astype(BF)
        sl_ref[pl.ds(base + CPAD, CPAD), :] = even.astype(BF)
        sl_ref[pl.ds(base + 2 * CPAD, CPAD), :] = odd.astype(BF)
        sl_ref[pl.ds(base + 3 * CPAD, CPAD), :] = pltpu.roll(even, 255, 1).astype(BF)
        first = jnp.where(lane == y, pltpu.roll(even[:, :128], y, 1), first)
        last = jnp.where(lane == y, pltpu.roll(odd[:, 128:], y + 1, 1), last)
        return first, last

    empty = jnp.zeros((CPAD, 128), F32)
    first, last = lax.fori_loop(0, ROWS, spread, (empty, empty))
    cols_ref[0] = first.astype(BF)
    cols_ref[1] = last.astype(BF)
    pl.semaphore_wait(barrier, 8)
    routes = [
        (cols_ref.at[1], colr_ref.at[0], (lat, right)),
        (cols_ref.at[0], colr_ref.at[1], (lat, left)),
        (cols_ref.at[1], colr_ref.at[2], (down, right)),
        (cols_ref.at[0], colr_ref.at[3], (down, left)),
        (cols_ref.at[1], colr_ref.at[4], (up, right)),
        (cols_ref.at[0], colr_ref.at[5], (up, left)),
        (sl_ref.at[pl.ds(ROWS * SLAB + CPAD, 2 * CPAD)], rowr_ref.at[0], (down, lon)),
        (sl_ref.at[pl.ds(SLAB + CPAD, 2 * CPAD)], rowr_ref.at[1], (up, lon)),
    ]
    copies = [
        remote(src, dst, send_sem.at[i], recv_sem.at[i], target)
        for i, (src, dst, target) in enumerate(routes)
    ]
    for i in (6, 7, 0, 1, 2, 3, 4, 5):
        copies[i].start()

    wf_ref[...] = sw_ref[...].astype(F32)
    for q in range(16):
        part = wf_ref[pl.ds(q * CHAN, CHAN), :]
        part = jnp.concatenate([part, jnp.zeros((CPAD - CHAN, D), F32)], axis=0)
        wp_ref[pl.ds(q * CPAD, CPAD), :] = part.astype(BF)
    for q in range(5):
        wt_ref[:, pl.ds(q * 256, 256)] = wp_ref[pl.ds(q * 256, 256), :].T
    wvt_ref[...] = kvw_ref[:, D:].T
    latents = latents_ref[...]
    centred = latents - jnp.mean(latents, axis=-1, keepdims=True)
    variance = jnp.mean(centred * centred, axis=-1, keepdims=True)
    normed = (centred / jnp.sqrt(variance + 1e-05) * lgain_ref[...]).astype(BF)
    query = jnp.dot(normed, qw_ref[...], preferred_element_type=F32).astype(BF)
    turned = query.T
    for h in range(HEADS):
        mine = (h % 2) * HD
        qt_ref[h, mine:mine + HD, :] = turned[h * HD:(h + 1) * HD, :]
        qt_ref[h, HD - mine:2 * HD - mine, :] = jnp.zeros((HD, LAT), BF)

    for copy in copies:
        copy.wait()

    def patch(y, left_column, right_column, left_roll, right_roll, base):
        a = sl_ref[pl.ds(base, CPAD), 0:128].astype(F32)
        b = sl_ref[pl.ds(base + 3 * CPAD, CPAD), 128:256].astype(F32)
        low = pltpu.roll(left_column.astype(F32), left_roll, 1)
        high = pltpu.roll(right_column.astype(F32), right_roll, 1)
        sl_ref[pl.ds(base, CPAD), 0:128] = jnp.where(lane == 0, low, a).astype(BF)
        sl_ref[pl.ds(base + 3 * CPAD, CPAD), 128:256] = jnp.where(lane == 127, high, b).astype(BF)

    def mend(y, carry):
        base = pl.multiple_of((y + 1) * SLAB, SLAB)
        patch(y, colr_ref[0], colr_ref[1], lax.rem(128 - y, 128), 127 - y, base)
        return carry

    lax.fori_loop(0, ROWS, mend, 0)
    for index, (slab, y, inside) in enumerate([(0, ROWS - 1, lat > 0), (ROWS + 1, 0, lat < NLATD - 1)]):
        base = slab * SLAB
        keep = jnp.where(inside, 1.0, 0.0).astype(F32)
        even = rowr_ref[index, 0:CPAD, :].astype(F32) * keep
        odd = rowr_ref[index, CPAD:2 * CPAD, :].astype(F32) * keep
        sl_ref[pl.ds(base, CPAD), :] = pltpu.roll(odd, 1, 1).astype(BF)
        sl_ref[pl.ds(base + CPAD, CPAD), :] = even.astype(BF)
        sl_ref[pl.ds(base + 2 * CPAD, CPAD), :] = odd.astype(BF)
        sl_ref[pl.ds(base + 3 * CPAD, CPAD), :] = pltpu.roll(even, 255, 1).astype(BF)
        patch(
            y, colr_ref[2 + 2 * index].astype(F32) * keep, colr_ref[3 + 2 * index].astype(F32) * keep,
            (128 - y) % 128, 127 - y, base,
        )


def prep(field, sw, kvw, latents, lgain, qw):
    return pl.pallas_call(
        prep_kernel,
        out_shape=(
            jax.ShapeDtypeStruct(((ROWS + 2) * SLAB, TW), BF),
            jax.ShapeDtypeStruct((D, 16 * CPAD), BF),
            jax.ShapeDtypeStruct((D, D), BF),
            jax.ShapeDtypeStruct((HEADS, 2 * HD, LAT), BF),
        ),
        in_specs=[VM] * 6,
        out_specs=(VM,) * 4,
        scratch_shapes=[
            pltpu.VMEM((4, CPAD * ROWS, 128), F32),
            pltpu.VMEM((16 * CHAN, D), F32),
            pltpu.VMEM((16 * CPAD, D), BF),
            pltpu.VMEM((2, CPAD, 128), BF),
            pltpu.VMEM((6, CPAD, 128), BF),
            pltpu.VMEM((2, 2 * CPAD, TW), BF),
            pltpu.SemaphoreType.DMA((8,)),
            pltpu.SemaphoreType.DMA((8,)),
        ],
        compiler_params=pltpu.CompilerParams(
            collective_id=0, has_side_effects=True, vmem_limit_bytes=56 * 2**20
        ),
        name="prep",
    )(field, sw, kvw, latents, lgain, qw)


def token_kernel(low_ref, high_ref, wt_ref, bias_ref, gain_ref, kvw_ref, wvt_ref, tok_ref, k_ref, vt_ref):
    window = jnp.concatenate([low_ref[...], high_ref[...]], axis=0)
    stem = jnp.dot(wt_ref[...], window, preferred_element_type=F32) + bias_ref[...]
    centred = stem - jnp.mean(stem, axis=0, keepdims=True)
    variance = jnp.mean(centred * centred, axis=0, keepdims=True)
    turned = (centred / jnp.sqrt(variance + 1e-05) * gain_ref[...]).astype(BF)
    tokens = turned.T
    tok_ref[0] = tokens
    keys = jnp.dot(tokens, kvw_ref[...], preferred_element_type=F32).astype(BF)
    for pair in range(HEADS // 2):
        k_ref[pair] = keys[:, pair * 128:(pair + 1) * 128]
    values = jnp.dot(wvt_ref[...], turned, preferred_element_type=F32).astype(BF)
    for h in range(HEADS):
        vt_ref[h, 0:HD, :] = values[h * HD:(h + 1) * HD, :]
        vt_ref[h, HD:EXT, :] = jnp.ones((EXT - HD, TW), BF)


def tokenise(slabs, wt, bias, gain, kvw, wvt):
    fixed = lambda shape: pl.BlockSpec(shape, lambda r: (0,) * len(shape))
    return pl.pallas_call(
        token_kernel,
        grid=(TH,),
        out_shape=(
            jax.ShapeDtypeStruct((TH, TW, D), BF),
            jax.ShapeDtypeStruct((HEADS // 2, TOK, 128), BF),
            jax.ShapeDtypeStruct((HEADS, EXT, TOK), BF),
        ),
        in_specs=[
            pl.BlockSpec((2 * SLAB, TW), lambda r: (r, 0)),
            pl.BlockSpec((2 * SLAB, TW), lambda r: (r + 1, 0)),
            fixed((D, 16 * CPAD)),
            fixed((D, 1)),
            fixed((D, 1)),
            fixed((D, D)),
            fixed((D, D)),
        ],
        out_specs=(
            pl.BlockSpec((1, TW, D), lambda r: (r, 0, 0)),
            pl.BlockSpec((HEADS // 2, TW, 128), lambda r: (0, r, 0)),
            pl.BlockSpec((HEADS, EXT, TW), lambda r: (0, 0, r)),
        ),
        compiler_params=pltpu.CompilerParams(vmem_limit_bytes=56 * 2**20),
        name="tokenise",
    )(slabs, slabs, wt, bias, gain, kvw, wvt)


def attend_kernel(
    k_hbm, vt_hbm, qt_hbm, hg_ref, out_ref,
    k_ref, vt_ref, qt_ref, s_ref, mx_ref, acc_ref, src1, dst1, src2, dst2, att,
    in_sem, send1, recv1, send2, recv2, send3, recv3,
):
    lat = lax.axis_index("lat")
    lon = lax.axis_index("lon")
    barrier = pltpu.get_barrier_semaphore()
    lon_peer = lambda s: (lat, lax.rem(lon + s, NLOND))
    lat_peer = lambda s: (lax.rem(lat + s, NLATD), lon)
    for s in range(1, NLOND):
        pl.semaphore_signal(barrier, inc=1, device_id=lon_peer(s), device_id_type=MESH)
    for s in range(1, NLATD):
        pl.semaphore_signal(barrier, inc=1, device_id=lat_peer(s), device_id_type=MESH)

    qt_copy = pltpu.make_async_copy(qt_hbm, qt_ref, in_sem.at[12])
    k_copies = [pltpu.make_async_copy(k_hbm.at[p], k_ref.at[p], in_sem.at[p]) for p in range(HEADS // 2)]
    v_copies = [pltpu.make_async_copy(vt_hbm.at[h], vt_ref.at[h], in_sem.at[4 + h]) for h in range(HEADS)]
    qt_copy.start()
    k_copies[0].start()
    v_copies[0].start()
    v_copies[1].start()
    for p in range(1, HEADS // 2):
        k_copies[p].start()
        v_copies[2 * p].start()
        v_copies[2 * p + 1].start()

    log2e = 1.4426950408889634
    scale = lambda h: hg_ref[h] * (log2e / 8.0)

    def score(h, j):
        at = pl.ds(pl.multiple_of(j * CH, CH), CH)
        s = jnp.dot(k_ref[h // 2, at, :], qt_ref[h], preferred_element_type=F32)
        s_ref[h % 2, at, :] = s
        mx_ref[h % 2] = jnp.maximum(mx_ref[h % 2], jnp.max(s.reshape(CH // 8, 8, LAT), axis=0))

    def weigh(h, j, top):
        at = pl.ds(pl.multiple_of(j * CH, CH), CH)
        p = jnp.exp2(s_ref[h % 2, at, :] * scale(h) - top).astype(BF)
        acc_ref[...] += jnp.dot(vt_ref[h, :, at], p, preferred_element_type=F32)

    def stat_rows(top, total):
        row = lax.broadcasted_iota(jnp.int32, (16, 128), 0)
        high = total.astype(BF).astype(F32)
        out = jnp.zeros((16, 128), F32)
        for n, value in enumerate((top, high, total - high)):
            out = jnp.where(row == 2 * n, value[:, :128], out)
            out = jnp.where(row == 2 * n + 1, value[:, 128:], out)
        return out.astype(BF)

    def merge(buffer, h, count):
        stats = [buffer[h, s, :, 256:384].astype(F32) for s in range(count)]
        tops = [jnp.concatenate([x[0:1], x[1:2]], axis=1) for x in stats]
        totals = [jnp.concatenate([x[2:3] + x[4:5], x[3:4] + x[5:6]], axis=1) for x in stats]
        top = functools.reduce(jnp.maximum, tops)
        total = jnp.zeros((1, 256), F32)
        acc = jnp.zeros((16, 256), F32)
        for s in range(count):
            fold = jnp.exp2(tops[s] - top)
            total = total + totals[s] * fold
            acc = acc + buffer[h, s, :, 0:256].astype(F32) * fold
        return top, total, acc

    def stage1(h, top):
        acc = acc_ref[...]
        total = acc[HD:HD + 1, :]
        stats = [stat_rows(top[:, g * 256:(g + 1) * 256], total[:, g * 256:(g + 1) * 256]) for g in range(2)]
        for p in range(NLOND):
            e, g = p % 4, p // 4
            src1[h, p, :, 0:256] = acc[16 * e:16 * e + 16, g * 256:(g + 1) * 256].astype(BF)
            src1[h, p, :, 256:384] = stats[g]
        dst1[h, 0] = src1[h, lon]
        for s in range(1, NLOND):
            remote(src1.at[h, lax.rem(lon + s, NLOND)], dst1.at[h, s], send1.at[h], recv1.at[h], lon_peer(s)).start()

    def wait(ref, sem):
        pltpu.make_async_copy(ref, ref, sem).wait()

    def stage2(h):
        wait(dst1.at[h, pl.ds(1, NLOND - 1)], recv1.at[h])
        top, total, acc = merge(dst1, h, NLOND)
        stats = stat_rows(top, total)
        src2[h, :, 0:256] = acc.astype(BF)
        src2[h, :, 256:384] = stats
        dst2[h, 0, :, 0:256] = acc.astype(BF)
        dst2[h, 0, :, 256:384] = stats
        for s in range(1, NLATD):
            remote(src2.at[h], dst2.at[h, s], send2.at[h], recv2.at[h], lat_peer(s)).start()

    e_at = lax.rem(lon, 4) * 16
    g_at = pl.multiple_of(lon // 4 * 256, 256)

    def stage3(h):
        wait(dst2.at[h, pl.ds(1, NLATD - 1)], recv2.at[h])
        top, total, acc = merge(dst2, h, NLATD)
        here = att.at[pl.ds(pl.multiple_of(h * HD + e_at, 16), 16), pl.ds(g_at, 256)]
        here[...] = (acc / total).astype(BF)
        for s in range(1, NLOND):
            remote(here, here, send3.at[h], recv3.at[h], lon_peer(s)).start()

    for h in range(HEADS + 1):
        slot = h % 2
        if h < HEADS:
            if h == 0:
                qt_copy.wait()
            if h % 2 == 0:
                k_copies[h // 2].wait()
            mx_ref[slot] = jnp.full((8, LAT), -jnp.inf, F32)
        if h > 0:
            v_copies[h - 1].wait()
            peak = jnp.max(mx_ref[1 - slot], axis=0, keepdims=True) * scale(h - 1)
            top = (peak + jnp.abs(peak) * 2.0**-7).astype(BF).astype(F32)
            acc_ref[...] = jnp.zeros_like(acc_ref)

        def both(j, carry):
            if h < HEADS:
                score(h, j)
            if h > 0:
                weigh(h - 1, j, top)
            return carry

        lax.fori_loop(0, TOK // CH, both, 0)
        if h == 1:
            pl.semaphore_wait(barrier, NLOND + NLATD - 2)
        if h > 0:
            stage1(h - 1, top)
        if h > 1:
            stage2(h - 2)
        if h > 2:
            stage3(h - 3)
    stage2(HEADS - 1)
    stage3(HEADS - 2)
    stage3(HEADS - 1)
    for h in range(HEADS):
        wait(att.at[pl.ds(0, 112), pl.ds(0, 256)], recv3.at[h])
        wait(dst1.at[h, pl.ds(1, NLOND - 1)], send1.at[h])
        wait(dst2.at[h, pl.ds(1, NLATD - 1)], send2.at[h])
        wait(att.at[pl.ds(0, 112), pl.ds(0, 256)], send3.at[h])
    out_ref[...] = att[...]


def attend(k, vt, qt, hg):
    return pl.pallas_call(
        attend_kernel,
        out_shape=jax.ShapeDtypeStruct((D, LAT), BF),
        in_specs=[ANY, ANY, ANY, SM],
        out_specs=VM,
        scratch_shapes=[
            pltpu.VMEM((HEADS // 2, TOK, 128), BF),
            pltpu.VMEM((HEADS, EXT, TOK), BF),
            pltpu.VMEM((HEADS, 2 * HD, LAT), BF),
            pltpu.VMEM((2, TOK, LAT), F32),
            pltpu.VMEM((2, 8, LAT), F32),
            pltpu.VMEM((EXT, LAT), F32),
            pltpu.VMEM((HEADS, NLOND, 16, 384), BF),
            pltpu.VMEM((HEADS, NLOND, 16, 384), BF),
            pltpu.VMEM((HEADS, 16, 384), BF),
            pltpu.VMEM((HEADS, NLATD, 16, 384), BF),
            pltpu.VMEM((D, LAT), BF),
            pltpu.SemaphoreType.DMA((13,)),
        ] + [pltpu.SemaphoreType.DMA((HEADS,))] * 6,
        compiler_params=pltpu.CompilerParams(
            collective_id=1, has_side_effects=True, vmem_limit_bytes=56 * 2**20
        ),
        name="attend",
    )(k, vt, qt, hg)


def mix_kernel(att_ref, ow_ref, gain_ref, out_ref):
    mixed = lax.dot_general(
        att_ref[...], ow_ref[...], (((0,), (0,)), ((), ())), preferred_element_type=F32
    )
    centred = mixed - jnp.mean(mixed, axis=-1, keepdims=True)
    variance = jnp.mean(centred * centred, axis=-1, keepdims=True)
    out_ref[...] = centred / jnp.sqrt(variance + 1e-05) * gain_ref[...]


def mix(att, ow, gain):
    return pl.pallas_call(
        mix_kernel,
        out_shape=jax.ShapeDtypeStruct((LAT, D), F32),
        in_specs=[VM] * 3,
        out_specs=VM,
        name="mix",
    )(att, ow, gain)


def shards(
    field, stem_weight, stem_bias, token_gain, kv_weight, latents, latent_gain,
    query_weight, head_gain, out_weight, out_gain,
):
    slabs, wt, wvt, qt = prep(field, stem_weight, kv_weight, latents, latent_gain.reshape(1, D), query_weight)
    tokens, k, vt = tokenise(
        slabs, wt, stem_bias.reshape(D, 1), token_gain.reshape(D, 1), kv_weight, wvt
    )
    att = attend(k, vt, qt, head_gain)
    return tokens, mix(att, out_weight, out_gain.reshape(1, D))


def solution(mesh):
    return jax.shard_map(
        shards,
        mesh=mesh,
        in_specs=(P(None, "lat", "lon"), P(), P(), P(), P(), P(), P(), P(), P(), P(), P()),
        out_specs=(P("lat", "lon", None), P()),
        check_vma=False,
    )
```

profile of v0, /device:TPU:1, one launch (start us, length us, event | category | flops | bytes accessed | tf_op | source)
XLA Modules:
  0.0 114.1 jit_solution(6128565481656470865)
XLA Ops:
  0.6 1.5 %copy.13.bias_ref = f32[512,1]{1,0:T(8,128)} copy(f32[512,1]{0,1:T(1,128)} %bitcast.4) | data formatting | bytes 4096 | tf_op jit(solution)/shard_map/reshape | solution.py:421
  2.2 1.5 %copy.14.gain_ref = f32[512,1]{1,0:T(8,128)} copy(f32[512,1]{0,1:T(1,128)} %bitcast.5) | data formatting | bytes 4096 | tf_op jit(solution)/shard_map/reshape | solution.py:421
  3.7 29.6 %prep.1 = (bf16[10880,256]{1,0:T(8,128)(2,1)}, bf16[512,1280]{1,0:T(8,128)(2,1)}, bf16[512,512]{1,0:T(8,128)(2,1)}, bf16[8,128,512]{2,1,0:T(8,128)(2,1)}) custom-call(bf16[69,32,512]{2,1,0:T(8,128)(2,1)} %field_ref.1, bf16[1104,512]{1,0:T(8,128)(2,1)} %sw_ref.1, bf16[512,1024]{1,0:T(8,128)(2,1)} %kvw_ref.3, f32[512,512]{1,0:T(8,128)} %latents_ref.1, ...), custom_call_target="tpu_custom_call" | custom-call | tf_op jit(solution)/shard_map/prep/pallas_call | solution.py:155
  33.3 29.0 %tokenise.1 = (bf16[16,256,512]{2,1,0:T(8,128)(2,1)}, bf16[4,4096,128]{2,1,0:T(8,128)(2,1)}, bf16[8,80,4096]{2,1,0:T(8,128)(2,1)}) custom-call(bf16[10880,256]{1,0:T(8,128)(2,1)} %get-tuple-element.9.low_ref.high_ref, bf16[10880,256]{1,0:T(8,128)(2,1)} %get-tuple-element.9.low_ref.high_ref, bf16[512,1280]{1,0:T(8,128)(2,1)} %get-tuple-element.10.wt_ref, ...), custom_call_target="tpu_custom_call" | custom-call | tf_op jit(solution)/shard_map/tokenise/pallas_call | solution.py:201
  62.3 48.9 %attend.1.att_ref = bf16[512,512]{1,0:T(8,128)(2,1)} custom-call(bf16[4,4096,128]{2,1,0:T(8,128)(2,1)} %get-tuple-element.13.k_hbm, bf16[8,80,4096]{2,1,0:T(8,128)(2,1)} %get-tuple-element.14.vt_hbm, bf16[8,128,512]{2,1,0:T(8,128)(2,1)} %get-tuple-element.15.qt_hbm, f32[8]{0:T(128)} %hg_ref.1), custom_call_target="tpu_custom_call" | custom-call | tf_op jit(solution)/shard_map/attend/pallas_call | solution.py:370
  111.2 2.9 %mix.1 = f32[512,512]{1,0:T(8,128)} custom-call(bf16[512,512]{1,0:T(8,128)(2,1)} %attend.1.att_ref, bf16[512,512]{1,0:T(8,128)(2,1)} %ow_ref.1, f32[1,512]{1,0:T(1,128)} %bitcast.7), custom_call_target="tpu_custom_call" | custom-call | tf_op jit(solution)/shard_map/mix/pallas_call | solution.py:406
where the time goes:
time: 114 us
  Pallas kernels  110 us (96%)
  local copies, waits for them, and re-layouts  3.06 us (3%)
    pallas_call x1, Pallas kernels, attend(): pl.pallas_call(attend_kernel, out_shape=jax.ShapeDtypeStruct((D, LAT), BF...  48.9 us
    pallas_call x1, Pallas kernels, prep(): pl.pallas_call(prep_kernel, out_shape=(jax.ShapeDtypeStruct(((ROWS + 2) *...  29.6 us
    pallas_call x1, Pallas kernels, tokenise(): pl.pallas_call(token_kernel, grid=(TH,), out_shape=(jax.ShapeDtypeStruct(...  29 us
    pallas_call x1, Pallas kernels, mix(): pl.pallas_call(mix_kernel, out_shape=jax.ShapeDtypeStruct((LAT, D), F32),...  2.88 us

commit v1 on v0

v1 whole, which is shorter than its diff:
```python
import functools

import jax
import jax.numpy as jnp
from jax import lax
from jax.experimental import pallas as pl
from jax.experimental.pallas import tpu as pltpu
from jax.sharding import PartitionSpec as P

HEADS = 8
HD = 64
LAT = 512
D = 512
CHAN = 69
CPAD = 80
ROWS = 32
COLS = 512
TH = 16
TW = 256
TOK = TH * TW
SLAB = 4 * CPAD
NLATD = 16
NLOND = 8
EXT = 80
CH = 2048
PITCH = 40
MESH = pl.DeviceIdType.MESH
F32 = jnp.float32
BF = jnp.bfloat16
VM = pl.BlockSpec(memory_space=pltpu.VMEM)
SM = pl.BlockSpec(memory_space=pltpu.SMEM)
ANY = pl.BlockSpec(memory_space=pl.ANY)


def remote(src, dst, send, recv, target):
    return pltpu.make_async_remote_copy(
        src_ref=src, dst_ref=dst, send_sem=send, recv_sem=recv, device_id=target, device_id_type=MESH
    )


def encode_kernel(
    field_hbm, sw_hbm, kvw_hbm, latents_hbm, qw_hbm, bias_ref, gain_ref, lgain_ref, hg_ref,
    tok_hbm, out_ref,
    field_ref, sw_ref, kvw_ref, latents_ref, qw_ref,
    sl_ref, wt_ref, wvt_ref, qt_ref, g_ref, wp_ref, cols_ref, colr_ref, rowr_ref,
    affine_ref, stem_ref, tok_ref,
    k_ref, vt_ref, s_ref, mx_ref, acc_ref, src1, dst1, src2, dst2, att,
    in_sem, tok_sem, edge_send, edge_recv, send1, recv1, send2, recv2, send3, recv3,
):
    lat = lax.axis_index("lat")
    lon = lax.axis_index("lon")
    up, down = lax.rem(lat + NLATD - 1, NLATD), lax.rem(lat + 1, NLATD)
    left, right = lax.rem(lon + NLOND - 1, NLOND), lax.rem(lon + 1, NLOND)
    loads = [
        pltpu.make_async_copy(src, dst, in_sem.at[i])
        for i, (src, dst) in enumerate([
            (field_hbm, field_ref), (sw_hbm, sw_ref), (kvw_hbm, kvw_ref), (latents_hbm, latents_ref), (qw_hbm, qw_ref),
        ])
    ]
    for load in loads:
        load.start()
    lon_peer = lambda s: (lat, lax.rem(lon + s, NLOND))
    lat_peer = lambda s: (lax.rem(lat + s, NLATD), lon)
    barrier = pltpu.get_barrier_semaphore()
    around = [(up, left), (up, right), (down, left), (down, right)]
    around += [lon_peer(s) for s in range(1, NLOND)] + [lat_peer(s) for s in range(1, NLATD)]
    for target in around:
        pl.semaphore_signal(barrier, inc=1, device_id=target, device_id_type=MESH)

    source = lax.broadcasted_iota(jnp.int32, (256, 256), 0)
    place = lax.broadcasted_iota(jnp.int32, (256, 256), 1)
    wanted = jnp.where(place < 128, 2 * place, 2 * (place - 128) + 1)
    select = (source == wanted).astype(F32).astype(BF)
    loads[0].wait()
    for half in range(2):
        block = field_ref[:, :, half * 256:(half + 1) * 256].reshape(CHAN * ROWS, 256)
        both = jnp.dot(block, select, preferred_element_type=F32)
        for c in range(CHAN):
            rows = both[c * ROWS:(c + 1) * ROWS]
            g_ref[half, c * PITCH:c * PITCH + ROWS, :] = rows[:, :128]
            g_ref[2 + half, c * PITCH:c * PITCH + ROWS, :] = rows[:, 128:]
    g_ref[:, CHAN * PITCH:CPAD * PITCH, :] = jnp.zeros((4, (CPAD - CHAN) * PITCH, 128), F32)

    lane = lax.broadcasted_iota(jnp.int32, (CPAD, 128), 1)

    def spread(y, carry):
        first, last = carry
        quarter = [g_ref[n, pl.ds(y, CPAD, stride=PITCH), :] for n in range(4)]
        even = jnp.concatenate(quarter[:2], axis=1)
        odd = jnp.concatenate(quarter[2:], axis=1)
        base = pl.multiple_of((y + 1) * SLAB, SLAB)
        sl_ref[pl.ds(base, CPAD), :] = pltpu.roll(odd, 1, 1).astype(BF)
        sl_ref[pl.ds(base + CPAD, CPAD), :] = even.astype(BF)
        sl_ref[pl.ds(base + 2 * CPAD, CPAD), :] = odd.astype(BF)
        sl_ref[pl.ds(base + 3 * CPAD, CPAD), :] = pltpu.roll(even, 255, 1).astype(BF)
        first = jnp.where(lane == y, pltpu.roll(even[:, :128], y, 1), first)
        last = jnp.where(lane == y, pltpu.roll(odd[:, 128:], y + 1, 1), last)
        return first, last

    empty = jnp.zeros((CPAD, 128), F32)
    first, last = lax.fori_loop(0, ROWS, spread, (empty, empty), unroll=2)
    cols_ref[0] = first.astype(BF)
    cols_ref[1] = last.astype(BF)
    pl.semaphore_wait(barrier, len(around))
    routes = [
        (cols_ref.at[1], colr_ref.at[0], (lat, right)),
        (cols_ref.at[0], colr_ref.at[1], (lat, left)),
        (cols_ref.at[1], colr_ref.at[2], (down, right)),
        (cols_ref.at[0], colr_ref.at[3], (down, left)),
        (cols_ref.at[1], colr_ref.at[4], (up, right)),
        (cols_ref.at[0], colr_ref.at[5], (up, left)),
        (sl_ref.at[pl.ds(ROWS * SLAB + CPAD, 2 * CPAD)], rowr_ref.at[0], (down, lon)),
        (sl_ref.at[pl.ds(SLAB + CPAD, 2 * CPAD)], rowr_ref.at[1], (up, lon)),
    ]
    copies = [
        remote(src, dst, edge_send.at[i], edge_recv.at[i], target)
        for i, (src, dst, target) in enumerate(routes)
    ]
    for i in (6, 7, 0, 1, 2, 3, 4, 5):
        copies[i].start()

    for load in loads[1:]:
        load.wait()
    for n in range(4):
        g_ref[n, 0:16 * CHAN, :] = sw_ref[:, n * 128:(n + 1) * 128].astype(F32)
        for q in range(16):
            part = g_ref[n, pl.ds(q * CHAN, CHAN), :]
            part = jnp.concatenate([part, jnp.zeros((CPAD - CHAN, 128), F32)], axis=0)
            wp_ref[pl.ds(q * CPAD, CPAD), n * 128:(n + 1) * 128] = part.astype(BF)
    for n, ref in enumerate((bias_ref, gain_ref)):
        affine_ref[n] = jnp.broadcast_to(ref[...], (128, D)).T
    for q in range(5):
        wt_ref[:, pl.ds(q * 256, 256)] = wp_ref[pl.ds(q * 256, 256), :].T
    wvt_ref[...] = kvw_ref[:, D:].T
    latents = latents_ref[...]
    centred = latents - jnp.mean(latents, axis=-1, keepdims=True)
    variance = jnp.mean(centred * centred, axis=-1, keepdims=True)
    normed = (centred / jnp.sqrt(variance + 1e-05) * lgain_ref[...]).astype(BF)
    query = jnp.dot(normed, qw_ref[...], preferred_element_type=F32).astype(BF)
    turned = query.T
    for h in range(HEADS):
        mine = (h % 2) * HD
        qt_ref[h, mine:mine + HD, :] = turned[h * HD:(h + 1) * HD, :]
        qt_ref[h, HD - mine:2 * HD - mine, :] = jnp.zeros((HD, LAT), BF)

    for copy in copies:
        copy.wait()

    def patch(y, left_column, right_column, left_roll, right_roll, base):
        a = sl_ref[pl.ds(base, CPAD), 0:128].astype(F32)
        b = sl_ref[pl.ds(base + 3 * CPAD, CPAD), 128:256].astype(F32)
        low = pltpu.roll(left_column.astype(F32), left_roll, 1)
        high = pltpu.roll(right_column.astype(F32), right_roll, 1)
        sl_ref[pl.ds(base, CPAD), 0:128] = jnp.where(lane == 0, low, a).astype(BF)
        sl_ref[pl.ds(base + 3 * CPAD, CPAD), 128:256] = jnp.where(lane == 127, high, b).astype(BF)

    def mend(y, carry):
        base = pl.multiple_of((y + 1) * SLAB, SLAB)
        patch(y, colr_ref[0], colr_ref[1], lax.rem(128 - y, 128), 127 - y, base)
        return carry

    lax.fori_loop(0, ROWS, mend, 0, unroll=4)
    for index, (slab, y, inside) in enumerate([(0, ROWS - 1, lat > 0), (ROWS + 1, 0, lat < NLATD - 1)]):
        base = slab * SLAB
        keep = jnp.where(inside, 1.0, 0.0).astype(F32)
        even = rowr_ref[index, 0:CPAD, :].astype(F32) * keep
        odd = rowr_ref[index, CPAD:2 * CPAD, :].astype(F32) * keep
        sl_ref[pl.ds(base, CPAD), :] = pltpu.roll(odd, 1, 1).astype(BF)
        sl_ref[pl.ds(base + CPAD, CPAD), :] = even.astype(BF)
        sl_ref[pl.ds(base + 2 * CPAD, CPAD), :] = odd.astype(BF)
        sl_ref[pl.ds(base + 3 * CPAD, CPAD), :] = pltpu.roll(even, 255, 1).astype(BF)
        patch(
            y, colr_ref[2 + 2 * index].astype(F32) * keep, colr_ref[3 + 2 * index].astype(F32) * keep,
            (128 - y) % 128, 127 - y, base,
        )

    def stem(r, slot):
        window = sl_ref[pl.ds(pl.multiple_of(r * 2 * SLAB, 2 * SLAB), 4 * SLAB), :]
        stem_ref[slot] = jnp.dot(wt_ref[...], window, preferred_element_type=F32)

    def finish(r, slot):
        wide = lambda n: jnp.concatenate([affine_ref[n]] * 2, axis=1)
        value = stem_ref[slot] + wide(0)
        centred = value - jnp.mean(value, axis=0, keepdims=True)
        variance = jnp.mean(centred * centred, axis=0, keepdims=True)
        turned = (centred * (1.0 / jnp.sqrt(variance + 1e-05)) * wide(1)).astype(BF)
        tokens = turned.T
        tok_ref[r] = tokens
        pltpu.make_async_copy(tok_ref.at[r], tok_hbm.at[r], tok_sem.at[r]).start()
        at = pl.ds(pl.multiple_of(r * TW, TW), TW)
        keys = jnp.dot(tokens, kvw_ref[:, 0:D], preferred_element_type=F32).astype(BF)
        for pair in range(HEADS // 2):
            k_ref[pair, at, :] = keys[:, pair * 128:(pair + 1) * 128]
        values = jnp.dot(wvt_ref[...], turned, preferred_element_type=F32).astype(BF)
        for h in range(HEADS):
            vt_ref[h, 0:HD, at] = values[h * HD:(h + 1) * HD, :]
            vt_ref[h, HD:EXT, at] = jnp.ones((EXT - HD, TW), BF)

    stem(0, 0)

    def two(i, carry):
        stem(2 * i + 1, 1)
        finish(2 * i, 0)
        stem(jnp.minimum(2 * i + 2, TH - 1), 0)
        finish(2 * i + 1, 1)
        return carry

    lax.fori_loop(0, TH // 2, two, 0)

    log2e = 1.4426950408889634
    scale = lambda h: hg_ref[h] * (log2e / 8.0)

    def score(h, j):
        at = pl.ds(pl.multiple_of(j * CH, CH), CH)
        s = jnp.dot(k_ref[h // 2, at, :], qt_ref[h], preferred_element_type=F32)
        s_ref[h % 2, at, :] = s
        mx_ref[h % 2] = jnp.maximum(mx_ref[h % 2], jnp.max(s.reshape(CH // 8, 8, LAT), axis=0))

    def weigh(h, j, top):
        at = pl.ds(pl.multiple_of(j * CH, CH), CH)
        p = jnp.exp2(s_ref[h % 2, at, :] * scale(h) - top).astype(BF)
        acc_ref[...] += jnp.dot(vt_ref[h, :, at], p, preferred_element_type=F32)

    def stat_rows(top, total):
        row = lax.broadcasted_iota(jnp.int32, (16, 128), 0)
        high = total.astype(BF).astype(F32)
        out = jnp.zeros((16, 128), F32)
        for n, value in enumerate((top, high, total - high)):
            out = jnp.where(row == 2 * n, value[:, :128], out)
            out = jnp.where(row == 2 * n + 1, value[:, 128:], out)
        return out.astype(BF)

    def merge(buffer, h, count):
        stats = [buffer[h, s, :, 256:384].astype(F32) for s in range(count)]
        tops = [jnp.concatenate([x[0:1], x[1:2]], axis=1) for x in stats]
        totals = [jnp.concatenate([x[2:3] + x[4:5], x[3:4] + x[5:6]], axis=1) for x in stats]
        top = functools.reduce(jnp.maximum, tops)
        total = jnp.zeros((1, 256), F32)
        acc = jnp.zeros((16, 256), F32)
        for s in range(count):
            fold = jnp.exp2(tops[s] - top)
            total = total + totals[s] * fold
            acc = acc + buffer[h, s, :, 0:256].astype(F32) * fold
        return top, total, acc

    def stage1(h, top):
        acc = acc_ref[...]
        total = acc[HD:HD + 1, :]
        stats = [stat_rows(top[:, g * 256:(g + 1) * 256], total[:, g * 256:(g + 1) * 256]) for g in range(2)]
        for p in range(NLOND):
            e, g = p % 4, p // 4
            src1[h, p, :, 0:256] = acc[16 * e:16 * e + 16, g * 256:(g + 1) * 256].astype(BF)
            src1[h, p, :, 256:384] = stats[g]
        dst1[h, 0] = src1[h, lon]
        for s in range(1, NLOND):
            remote(src1.at[h, lax.rem(lon + s, NLOND)], dst1.at[h, s], send1.at[h], recv1.at[h], lon_peer(s)).start()

    def wait(ref, sem):
        pltpu.make_async_copy(ref, ref, sem).wait()

    def stage2(h):
        wait(dst1.at[h, pl.ds(1, NLOND - 1)], recv1.at[h])
        top, total, acc = merge(dst1, h, NLOND)
        stats = stat_rows(top, total)
        src2[h, :, 0:256] = acc.astype(BF)
        src2[h, :, 256:384] = stats
        dst2[h, lat, :, 0:256] = acc.astype(BF)
        dst2[h, lat, :, 256:384] = stats
        for s in range(1, NLATD):
            remote(src2.at[h], dst2.at[h, lat], send2.at[h], recv2.at[h], lat_peer(s)).start()

    e_at = lax.rem(lon, 4) * 16
    g_at = pl.multiple_of(lon // 4 * 256, 256)

    def stage3(h):
        wait(dst2.at[h, pl.ds(1, NLATD - 1)], recv2.at[h])
        top, total, acc = merge(dst2, h, NLATD)
        here = att.at[pl.ds(pl.multiple_of(h * HD + e_at, 16), 16), pl.ds(g_at, 256)]
        here[...] = (acc / total).astype(BF)
        for s in range(1, NLOND):
            remote(here, here, send3.at[h], recv3.at[h], lon_peer(s)).start()

    for h in range(HEADS + 1):
        slot = h % 2
        if h < HEADS:
            mx_ref[slot] = jnp.full((8, LAT), -jnp.inf, F32)
        if h > 0:
            peak = jnp.max(mx_ref[1 - slot], axis=0, keepdims=True) * scale(h - 1)
            top = (peak + jnp.abs(peak) * 2.0**-7).astype(BF).astype(F32)
            acc_ref[...] = jnp.zeros_like(acc_ref)

        def both(j, carry):
            if h < HEADS:
                score(h, j)
            if h > 0:
                weigh(h - 1, j, top)
            return carry

        lax.fori_loop(0, TOK // CH, both, 0)
        if h > 0:
            stage1(h - 1, top)
        if h > 2:
            stage2(h - 3)
        if h > 5:
            stage3(h - 6)
    stage2(6)
    stage3(3)
    stage3(4)
    stage2(7)
    stage3(5)
    stage3(6)
    stage3(7)
    for r in range(TH):
        wait(tok_ref.at[r], tok_sem.at[r])
    for h in range(HEADS):
        wait(att.at[pl.ds(0, 112), pl.ds(0, 256)], recv3.at[h])
        wait(dst1.at[h, pl.ds(1, NLOND - 1)], send1.at[h])
        wait(dst2.at[h, pl.ds(1, NLATD - 1)], send2.at[h])
        wait(att.at[pl.ds(0, 112), pl.ds(0, 256)], send3.at[h])
    out_ref[...] = att[...]


def encode(field, sw, kvw, latents, qw, bias, gain, lgain, hg):
    dma = pltpu.SemaphoreType.DMA
    return pl.pallas_call(
        encode_kernel,
        out_shape=(jax.ShapeDtypeStruct((TH, TW, D), BF), jax.ShapeDtypeStruct((D, LAT), BF)),
        in_specs=[ANY] * 5 + [VM] * 3 + [SM],
        out_specs=(ANY, VM),
        scratch_shapes=[
            pltpu.VMEM((CHAN, ROWS, COLS), BF),
            pltpu.VMEM((16 * CHAN, D), BF),
            pltpu.VMEM((D, 2 * D), BF),
            pltpu.VMEM((LAT, D), F32),
            pltpu.VMEM((D, D), BF),
            pltpu.VMEM(((ROWS + 2) * SLAB, TW), BF),
            pltpu.VMEM((D, 16 * CPAD), BF),
            pltpu.VMEM((D, D), BF),
            pltpu.VMEM((HEADS, 2 * HD, LAT), BF),
            pltpu.VMEM((4, CPAD * PITCH, 128), F32),
            pltpu.VMEM((16 * CPAD, D), BF),
            pltpu.VMEM((2, CPAD, 128), BF),
            pltpu.VMEM((6, CPAD, 128), BF),
            pltpu.VMEM((2, 2 * CPAD, TW), BF),
            pltpu.VMEM((2, D, 128), F32),
            pltpu.VMEM((2, D, TW), F32),
            pltpu.VMEM((TH, TW, D), BF),
            pltpu.VMEM((HEADS // 2, TOK, 128), BF),
            pltpu.VMEM((HEADS, EXT, TOK), BF),
            pltpu.VMEM((2, TOK, LAT), F32),
            pltpu.VMEM((2, 8, LAT), F32),
            pltpu.VMEM((EXT, LAT), F32),
            pltpu.VMEM((HEADS, NLOND, 16, 384), BF),
            pltpu.VMEM((HEADS, NLOND, 16, 384), BF),
            pltpu.VMEM((HEADS, 16, 384), BF),
            pltpu.VMEM((HEADS, NLATD, 16, 384), BF),
            pltpu.VMEM((D, LAT), BF),
            dma((5,)), dma((TH,)), dma((8,)), dma((8,)),
        ] + [dma((HEADS,))] * 6,
        compiler_params=pltpu.CompilerParams(
            collective_id=0, has_side_effects=True, vmem_limit_bytes=62 * 2**20
        ),
        name="encode",
    )(field, sw, kvw, latents, qw, bias, gain, lgain, hg)


def mix_kernel(tok_hbm, att_ref, ow_ref, gain_ref, tok_out, out_ref, sem):
    quarter = TH // 4
    copies = [
        pltpu.make_async_copy(tok_hbm.at[pl.ds(n * quarter, quarter)], tok_out.at[pl.ds(n * quarter, quarter)], sem.at[n])
        for n in range(4)
    ]
    for copy in copies:
        copy.start()
    mixed = lax.dot_general(
        att_ref[...], ow_ref[...], (((0,), (0,)), ((), ())), preferred_element_type=F32
    )
    centred = mixed - jnp.mean(mixed, axis=-1, keepdims=True)
    variance = jnp.mean(centred * centred, axis=-1, keepdims=True)
    out_ref[...] = centred / jnp.sqrt(variance + 1e-05) * gain_ref[...]
    for copy in copies:
        copy.wait()


def mix(tokens, att, ow, gain):
    return pl.pallas_call(
        mix_kernel,
        out_shape=(jax.ShapeDtypeStruct((TH, TW, D), BF), jax.ShapeDtypeStruct((LAT, D), F32)),
        in_specs=[ANY] + [VM] * 3,
        out_specs=(ANY, VM),
        scratch_shapes=[pltpu.SemaphoreType.DMA((4,))],
        compiler_params=pltpu.CompilerParams(vmem_limit_bytes=62 * 2**20),
        name="mix",
    )(tokens, att, ow, gain)


def shards(
    field, stem_weight, stem_bias, token_gain, kv_weight, latents, latent_gain,
    query_weight, head_gain, out_weight, out_gain,
):
    row = lambda x: x.reshape(1, D)
    tokens, att = encode(
        field, stem_weight, kv_weight, latents, query_weight, row(stem_bias), row(token_gain), row(latent_gain), head_gain
    )
    return mix(tokens, att, out_weight, row(out_gain))


def solution(mesh):
    return jax.shard_map(
        shards,
        mesh=mesh,
        in_specs=(P(None, "lat", "lon"), P(), P(), P(), P(), P(), P(), P(), P(), P(), P()),
        out_specs=(P("lat", "lon", None), P()),
        check_vma=False,
    )
```

time: 114 us -> 202 us (1.77)
  Pallas kernels: 110 us -> 201 us
  local copies, waits for them, and re-layouts: 3.06 us -> 0 us
    pallas_call x4 -> x2, Pallas kernels: 110 us -> 201 us  [the longest x1 130 us: mix(): pl.pallas_call(mix_kernel, out_shape=(jax.ShapeDtypeStruct((TH, TW, D), B...]
    reshape x2 -> x0, local copies, waits for them, and re-layouts: 3.06 us -> none  [the longest x1 1.53 us: shards(): stem_bias.reshape(D, 1)]
where the time goes in v1:
time: 202 us; the launch traced here: 201 us
  Pallas kernels  201 us (100%)
    pallas_call x1, Pallas kernels, mix(): pl.pallas_call(mix_kernel, out_shape=(jax.ShapeDtypeStruct((TH, TW, D), B...  130 us
    pallas_call x1, Pallas kernels, encode(): pl.pallas_call(encode_kernel, out_shape=(jax.ShapeDtypeStruct((TH, TW, D)...  70.3 us

profile of v1, /device:TPU:1, one launch (start us, length us, event | category | flops | bytes accessed | tf_op | source)
XLA Modules:
  0.0 201.5 jit_solution(13911904254892492362)
XLA Ops:
  0.6 70.3 %encode.1 = (bf16[16,256,512]{2,1,0:T(8,128)(2,1)}, bf16[512,512]{1,0:T(8,128)(2,1)}) custom-call(bf16[69,32,512]{2,1,0:T(8,128)(2,1)} %field_hbm.1, bf16[1104,512]{1,0:T(8,128)(2,1)} %sw_hbm.1, bf16[512,1024]{1,0:T(8,128)(2,1)} %kvw_hbm.1, f32[512,512]{1,0:T(8,128)} %latents_hbm.1, bf16[512,512]{1,0:T(8,128)(2,1)} %qw_hbm.1, f32[1,512]{1,0:T(1,128)} %bitcast.4, ...), custom_call_target="tpu_custom_call" | custom-call | tf_op jit(solution)/shard_map/encode/pallas_call | solution.py:325
  70.9 130.4 %mix.1 = (bf16[16,256,512]{2,1,0:T(8,128)(2,1)}, f32[512,512]{1,0:T(8,128)}) custom-call(bf16[16,256,512]{2,1,0:T(8,128)(2,1)} %get-tuple-element.4.tok_hbm, bf16[512,512]{1,0:T(8,128)(2,1)} %get-tuple-element.5.att_ref, bf16[512,512]{1,0:T(8,128)(2,1)} %ow_ref.1, f32[1,512]{1,0:T(1,128)} %bitcast.7), custom_call_target="tpu_custom_call" | custom-call | tf_op jit(solution)/shard_map/mix/pallas_call | solution.py:386

commit v2 on v1

--- a/solution.py
+++ b/solution.py
@@ -43,7 +43,7 @@
     tok_hbm, out_ref,
     field_ref, sw_ref, kvw_ref, latents_ref, qw_ref,
     sl_ref, wt_ref, wvt_ref, qt_ref, g_ref, wp_ref, cols_ref, colr_ref, rowr_ref,
-    affine_ref, stem_ref, tok_ref,
+    affine_ref, stem_ref, turned_ref, tok_ref,
     k_ref, vt_ref, s_ref, mx_ref, acc_ref, src1, dst1, src2, dst2, att,
     in_sem, tok_sem, edge_send, edge_recv, send1, recv1, send2, recv2, send3, recv3,
 ):
@@ -116,7 +116,7 @@
         remote(src, dst, edge_send.at[i], edge_recv.at[i], target)
         for i, (src, dst, target) in enumerate(routes)
     ]
-    for i in (6, 7, 0, 1, 2, 3, 4, 5):
+    for i in (0, 1, 6, 7, 2, 3, 4, 5):
         copies[i].start()
 
     for load in loads[1:]:
@@ -143,7 +143,7 @@
         qt_ref[h, mine:mine + HD, :] = turned[h * HD:(h + 1) * HD, :]
         qt_ref[h, HD - mine:2 * HD - mine, :] = jnp.zeros((HD, LAT), BF)
 
-    for copy in copies:
+    for copy in copies[:2]:
         copy.wait()
 
     def patch(y, left_column, right_column, left_roll, right_roll, base):
@@ -160,52 +160,81 @@
         return carry
 
     lax.fori_loop(0, ROWS, mend, 0, unroll=4)
-    for index, (slab, y, inside) in enumerate([(0, ROWS - 1, lat > 0), (ROWS + 1, 0, lat < NLATD - 1)]):
-        base = slab * SLAB
-        keep = jnp.where(inside, 1.0, 0.0).astype(F32)
-        even = rowr_ref[index, 0:CPAD, :].astype(F32) * keep
-        odd = rowr_ref[index, CPAD:2 * CPAD, :].astype(F32) * keep
-        sl_ref[pl.ds(base, CPAD), :] = pltpu.roll(odd, 1, 1).astype(BF)
-        sl_ref[pl.ds(base + CPAD, CPAD), :] = even.astype(BF)
-        sl_ref[pl.ds(base + 2 * CPAD, CPAD), :] = odd.astype(BF)
-        sl_ref[pl.ds(base + 3 * CPAD, CPAD), :] = pltpu.roll(even, 255, 1).astype(BF)
-        patch(
-            y, colr_ref[2 + 2 * index].astype(F32) * keep, colr_ref[3 + 2 * index].astype(F32) * keep,
-            (128 - y) % 128, 127 - y, base,
-        )
 
     def stem(r, slot):
         window = sl_ref[pl.ds(pl.multiple_of(r * 2 * SLAB, 2 * SLAB), 4 * SLAB), :]
         stem_ref[slot] = jnp.dot(wt_ref[...], window, preferred_element_type=F32)
 
-    def finish(r, slot):
+    def norm(r, slot):
         wide = lambda n: jnp.concatenate([affine_ref[n]] * 2, axis=1)
         value = stem_ref[slot] + wide(0)
         centred = value - jnp.mean(value, axis=0, keepdims=True)
         variance = jnp.mean(centred * centred, axis=0, keepdims=True)
         turned = (centred * (1.0 / jnp.sqrt(variance + 1e-05)) * wide(1)).astype(BF)
-        tokens = turned.T
-        tok_ref[r] = tokens
-        pltpu.make_async_copy(tok_ref.at[r], tok_hbm.at[r], tok_sem.at[r]).start()
+        turned_ref[slot] = turned
+        tok_ref[r] = turned.T
+
+    def project(r, slot):
         at = pl.ds(pl.multiple_of(r * TW, TW), TW)
-        keys = jnp.dot(tokens, kvw_ref[:, 0:D], preferred_element_type=F32).astype(BF)
+        keys = jnp.dot(tok_ref[r], kvw_ref[:, 0:D], preferred_element_type=F32).astype(BF)
         for pair in range(HEADS // 2):
             k_ref[pair, at, :] = keys[:, pair * 128:(pair + 1) * 128]
-        values = jnp.dot(wvt_ref[...], turned, preferred_element_type=F32).astype(BF)
+        values = jnp.dot(wvt_ref[...], turned_ref[slot], preferred_element_type=F32).astype(BF)
         for h in range(HEADS):
             vt_ref[h, 0:HD, at] = values[h * HD:(h + 1) * HD, :]
             vt_ref[h, HD:EXT, at] = jnp.ones((EXT - HD, TW), BF)
 
+    def ship(r):
+        pltpu.make_async_copy(tok_ref.at[r], tok_hbm.at[r], tok_sem.at[r]).start()
+
+    def border():
+        for copy in copies[2:]:
+            copy.wait()
+        for index, (slab, y, inside) in enumerate([(0, ROWS - 1, lat > 0), (ROWS + 1, 0, lat < NLATD - 1)]):
+            base = slab * SLAB
+            keep = jnp.where(inside, 1.0, 0.0).astype(F32)
+            even = rowr_ref[index, 0:CPAD, :].astype(F32) * keep
+            odd = rowr_ref[index, CPAD:2 * CPAD, :].astype(F32) * keep
+            sl_ref[pl.ds(base, CPAD), :] = pltpu.roll(odd, 1, 1).astype(BF)
+            sl_ref[pl.ds(base + CPAD, CPAD), :] = even.astype(BF)
+            sl_ref[pl.ds(base + 2 * CPAD, CPAD), :] = odd.astype(BF)
+            sl_ref[pl.ds(base + 3 * CPAD, CPAD), :] = pltpu.roll(even, 255, 1).astype(BF)
+            patch(
+                y, colr_ref[2 + 2 * index].astype(F32) * keep, colr_ref[3 + 2 * index].astype(F32) * keep,
+                (128 - y) % 128, 127 - y, base,
+            )
+
+    stem(1, 1)
+    norm(1, 1)
+    stem(2, 0)
+
+    def two(i, carry):
+        r = 2 * i + 1
+        ship(r)
+        project(r, 1)
+        norm(r + 1, 0)
+        stem(r + 2, 1)
+        ship(r + 1)
+        project(r + 1, 0)
+        norm(r + 2, 1)
+        stem(r + 3, 0)
+        return carry
+
+    lax.fori_loop(0, 6, two, 0)
+    border()
+    ship(13)
+    project(13, 1)
+    norm(14, 0)
+    stem(15, 1)
+    ship(14)
+    project(14, 0)
+    norm(15, 1)
     stem(0, 0)
-
-    def two(i, carry):
-        stem(2 * i + 1, 1)
-        finish(2 * i, 0)
-        stem(jnp.minimum(2 * i + 2, TH - 1), 0)
-        finish(2 * i + 1, 1)
-        return carry
-
-    lax.fori_loop(0, TH // 2, two, 0)
+    ship(15)
+    project(15, 1)
+    norm(0, 0)
+    ship(0)
+    project(0, 0)
 
     log2e = 1.4426950408889634
     scale = lambda h: hg_ref[h] * (log2e / 8.0)
@@ -344,6 +373,7 @@
             pltpu.VMEM((2, 2 * CPAD, TW), BF),
             pltpu.VMEM((2, D, 128), F32),
             pltpu.VMEM((2, D, TW), F32),
+            pltpu.VMEM((2, D, TW), BF),
             pltpu.VMEM((TH, TW, D), BF),
             pltpu.VMEM((HEADS // 2, TOK, 128), BF),
             pltpu.VMEM((HEADS, EXT, TOK), BF),
@@ -364,21 +394,23 @@
     )(field, sw, kvw, latents, qw, bias, gain, lgain, hg)
 
 
-def mix_kernel(tok_hbm, att_ref, ow_ref, gain_ref, tok_out, out_ref, sem):
-    quarter = TH // 4
-    copies = [
-        pltpu.make_async_copy(tok_hbm.at[pl.ds(n * quarter, quarter)], tok_out.at[pl.ds(n * quarter, quarter)], sem.at[n])
-        for n in range(4)
-    ]
-    for copy in copies:
+def mix_kernel(tok_hbm, att_ref, ow_ref, gain_ref, tok_out, out_ref, hold, in_sem, out_sem):
+    ins = [pltpu.make_async_copy(tok_hbm.at[pl.ds(2 * n, 2)], hold.at[pl.ds(2 * n, 2)], in_sem.at[n]) for n in range(TH // 2)]
+    outs = [pltpu.make_async_copy(hold.at[pl.ds(2 * n, 2)], tok_out.at[pl.ds(2 * n, 2)], out_sem.at[n]) for n in range(TH // 2)]
+    for copy in ins:
         copy.start()
-    mixed = lax.dot_general(
-        att_ref[...], ow_ref[...], (((0,), (0,)), ((), ())), preferred_element_type=F32
-    )
-    centred = mixed - jnp.mean(mixed, axis=-1, keepdims=True)
-    variance = jnp.mean(centred * centred, axis=-1, keepdims=True)
-    out_ref[...] = centred / jnp.sqrt(variance + 1e-05) * gain_ref[...]
-    for copy in copies:
+    weight = ow_ref[...]
+    for n in range(4):
+        for m in (2 * n, 2 * n + 1):
+            ins[m].wait()
+            outs[m].start()
+        mixed = lax.dot_general(
+            att_ref[:, n * 128:(n + 1) * 128], weight, (((0,), (0,)), ((), ())), preferred_element_type=F32
+        )
+        centred = mixed - jnp.mean(mixed, axis=-1, keepdims=True)
+        variance = jnp.mean(centred * centred, axis=-1, keepdims=True)
+        out_ref[n * 128:(n + 1) * 128, :] = centred / jnp.sqrt(variance + 1e-05) * gain_ref[...]
+    for copy in outs:
         copy.wait()
 
 
@@ -388,7 +420,7 @@
         out_shape=(jax.ShapeDtypeStruct((TH, TW, D), BF), jax.ShapeDtypeStruct((LAT, D), F32)),
         in_specs=[ANY] + [VM] * 3,
         out_specs=(ANY, VM),
-        scratch_shapes=[pltpu.SemaphoreType.DMA((4,))],
+        scratch_shapes=[pltpu.VMEM((TH, TW, D), BF)] + [pltpu.SemaphoreType.DMA((TH // 2,))] * 2,
         compiler_params=pltpu.CompilerParams(vmem_limit_bytes=62 * 2**20),
         name="mix",
     )(tokens, att, ow, gain)

time: 202 us -> 70.8 us (0.35)
  Pallas kernels: 201 us -> 69.8 us
    pallas_call x1, Pallas kernels: 130 us -> 5.8 us  [mix(): pl.pallas_call(mix_kernel, out_shape=(jax.ShapeDtypeStruct((TH, TW, D), B...]
    pallas_call x1, Pallas kernels: 70.3 us -> 64 us  [encode(): pl.pallas_call(encode_kernel, out_shape=(jax.ShapeDtypeStruct((TH, TW, D)...]
where the time goes in v2:
time: 70.8 us; the launch traced here: 70.6 us
  Pallas kernels  69.8 us (99%)
  between operations  0.8 us (1%)
    pallas_call x1, Pallas kernels, encode(): pl.pallas_call(encode_kernel, out_shape=(jax.ShapeDtypeStruct((TH, TW, D)...  64 us
    pallas_call x1, Pallas kernels, mix(): pl.pallas_call(mix_kernel, out_shape=(jax.ShapeDtypeStruct((TH, TW, D), B...  5.8 us

profile of v2, /device:TPU:1, one launch (start us, length us, event | category | flops | bytes accessed | tf_op | source)
XLA Modules:
  0.0 70.6 jit_solution(241597795978602979)
XLA Ops:
  0.6 64.0 %encode.1 = (bf16[16,256,512]{2,1,0:T(8,128)(2,1)}, bf16[512,512]{1,0:T(8,128)(2,1)}) custom-call(bf16[69,32,512]{2,1,0:T(8,128)(2,1)} %field_hbm.1, bf16[1104,512]{1,0:T(8,128)(2,1)} %sw_hbm.1, bf16[512,1024]{1,0:T(8,128)(2,1)} %kvw_hbm.1, f32[512,512]{1,0:T(8,128)} %latents_hbm.1, bf16[512,512]{1,0:T(8,128)(2,1)} %qw_hbm.1, f32[1,512]{1,0:T(1,128)} %bitcast.4, ...), custom_call_target="tpu_custom_call" | custom-call | tf_op jit(solution)/shard_map/encode/pallas_call | solution.py:354
  64.6 5.8 %mix.1 = (bf16[16,256,512]{2,1,0:T(8,128)(2,1)}, f32[512,512]{1,0:T(8,128)}) custom-call(bf16[16,256,512]{2,1,0:T(8,128)(2,1)} %get-tuple-element.4.tok_hbm, bf16[512,512]{1,0:T(8,128)(2,1)} %get-tuple-element.5.att_ref, bf16[512,512]{1,0:T(8,128)(2,1)} %ow_ref.1, f32[1,512]{1,0:T(1,128)} %bitcast.7), custom_call_target="tpu_custom_call" | custom-call | tf_op jit(solution)/shard_map/mix/pallas_call | solution.py:418

commit v3 on v2

--- a/solution.py
+++ b/solution.py
@@ -24,6 +24,7 @@
 EXT = 80
 CH = 2048
 PITCH = 40
+LIMIT = 58
 MESH = pl.DeviceIdType.MESH
 F32 = jnp.float32
 BF = jnp.bfloat16
@@ -40,12 +41,12 @@
 
 def encode_kernel(
     field_hbm, sw_hbm, kvw_hbm, latents_hbm, qw_hbm, bias_ref, gain_ref, lgain_ref, hg_ref,
-    tok_hbm, out_ref,
+    tok_ref, out_ref,
     field_ref, sw_ref, kvw_ref, latents_ref, qw_ref,
     sl_ref, wt_ref, wvt_ref, qt_ref, g_ref, wp_ref, cols_ref, colr_ref, rowr_ref,
-    affine_ref, stem_ref, turned_ref, tok_ref,
+    affine_ref, stem_ref, turned_ref,
     k_ref, vt_ref, s_ref, mx_ref, acc_ref, src1, dst1, src2, dst2, att,
-    in_sem, tok_sem, edge_send, edge_recv, send1, recv1, send2, recv2, send3, recv3,
+    in_sem, edge_send, edge_recv, send1, recv1, send2, recv2, send3, recv3,
 ):
     lat = lax.axis_index("lat")
     lon = lax.axis_index("lon")
@@ -184,9 +185,6 @@
             vt_ref[h, 0:HD, at] = values[h * HD:(h + 1) * HD, :]
             vt_ref[h, HD:EXT, at] = jnp.ones((EXT - HD, TW), BF)
 
-    def ship(r):
-        pltpu.make_async_copy(tok_ref.at[r], tok_hbm.at[r], tok_sem.at[r]).start()
-
     def border():
         for copy in copies[2:]:
             copy.wait()
@@ -210,11 +208,9 @@
 
     def two(i, carry):
         r = 2 * i + 1
-        ship(r)
         project(r, 1)
         norm(r + 1, 0)
         stem(r + 2, 1)
-        ship(r + 1)
         project(r + 1, 0)
         norm(r + 2, 1)
         stem(r + 3, 0)
@@ -222,18 +218,14 @@
 
     lax.fori_loop(0, 6, two, 0)
     border()
-    ship(13)
     project(13, 1)
     norm(14, 0)
     stem(15, 1)
-    ship(14)
     project(14, 0)
     norm(15, 1)
     stem(0, 0)
-    ship(15)
     project(15, 1)
     norm(0, 0)
-    ship(0)
     project(0, 0)
 
     log2e = 1.4426950408889634
@@ -339,8 +331,6 @@
     stage3(5)
     stage3(6)
     stage3(7)
-    for r in range(TH):
-        wait(tok_ref.at[r], tok_sem.at[r])
     for h in range(HEADS):
         wait(att.at[pl.ds(0, 112), pl.ds(0, 256)], recv3.at[h])
         wait(dst1.at[h, pl.ds(1, NLOND - 1)], send1.at[h])
@@ -353,9 +343,9 @@
     dma = pltpu.SemaphoreType.DMA
     return pl.pallas_call(
         encode_kernel,
-        out_shape=(jax.ShapeDtypeStruct((TH, TW, D), BF), jax.ShapeDtypeStruct((D, LAT), BF)),
+        out_shape=(pltpu.VMEM((TH, TW, D), BF), pltpu.VMEM((D, LAT), BF)),
         in_specs=[ANY] * 5 + [VM] * 3 + [SM],
-        out_specs=(ANY, VM),
+        out_specs=(VM, VM),
         scratch_shapes=[
             pltpu.VMEM((CHAN, ROWS, COLS), BF),
             pltpu.VMEM((16 * CHAN, D), BF),
@@ -374,7 +364,6 @@
             pltpu.VMEM((2, D, 128), F32),
             pltpu.VMEM((2, D, TW), F32),
             pltpu.VMEM((2, D, TW), BF),
-            pltpu.VMEM((TH, TW, D), BF),
             pltpu.VMEM((HEADS // 2, TOK, 128), BF),
             pltpu.VMEM((HEADS, EXT, TOK), BF),
             pltpu.VMEM((2, TOK, LAT), F32),
@@ -385,32 +374,28 @@
             pltpu.VMEM((HEADS, 16, 384), BF),
             pltpu.VMEM((HEADS, NLATD, 16, 384), BF),
             pltpu.VMEM((D, LAT), BF),
-            dma((5,)), dma((TH,)), dma((8,)), dma((8,)),
+            dma((5,)), dma((8,)), dma((8,)),
         ] + [dma((HEADS,))] * 6,
         compiler_params=pltpu.CompilerParams(
-            collective_id=0, has_side_effects=True, vmem_limit_bytes=62 * 2**20
+            collective_id=0, has_side_effects=True, vmem_limit_bytes=LIMIT * 2**20
         ),
         name="encode",
     )(field, sw, kvw, latents, qw, bias, gain, lgain, hg)
 
 
-def mix_kernel(tok_hbm, att_ref, ow_ref, gain_ref, tok_out, out_ref, hold, in_sem, out_sem):
-    ins = [pltpu.make_async_copy(tok_hbm.at[pl.ds(2 * n, 2)], hold.at[pl.ds(2 * n, 2)], in_sem.at[n]) for n in range(TH // 2)]
-    outs = [pltpu.make_async_copy(hold.at[pl.ds(2 * n, 2)], tok_out.at[pl.ds(2 * n, 2)], out_sem.at[n]) for n in range(TH // 2)]
-    for copy in ins:
+def mix_kernel(tok_in, att_ref, ow_ref, gain_ref, tok_out, out_ref, sem):
+    copies = [pltpu.make_async_copy(tok_in.at[pl.ds(4 * n, 4)], tok_out.at[pl.ds(4 * n, 4)], sem.at[n]) for n in range(4)]
+    for copy in copies:
         copy.start()
     weight = ow_ref[...]
     for n in range(4):
-        for m in (2 * n, 2 * n + 1):
-            ins[m].wait()
-            outs[m].start()
         mixed = lax.dot_general(
             att_ref[:, n * 128:(n + 1) * 128], weight, (((0,), (0,)), ((), ())), preferred_element_type=F32
         )
         centred = mixed - jnp.mean(mixed, axis=-1, keepdims=True)
         variance = jnp.mean(centred * centred, axis=-1, keepdims=True)
         out_ref[n * 128:(n + 1) * 128, :] = centred / jnp.sqrt(variance + 1e-05) * gain_ref[...]
-    for copy in outs:
+    for copy in copies:
         copy.wait()
 
 
@@ -420,8 +405,8 @@
         out_shape=(jax.ShapeDtypeStruct((TH, TW, D), BF), jax.ShapeDtypeStruct((LAT, D), F32)),
         in_specs=[ANY] + [VM] * 3,
         out_specs=(ANY, VM),
-        scratch_shapes=[pltpu.VMEM((TH, TW, D), BF)] + [pltpu.SemaphoreType.DMA((TH // 2,))] * 2,
-        compiler_params=pltpu.CompilerParams(vmem_limit_bytes=62 * 2**20),
+        scratch_shapes=[pltpu.SemaphoreType.DMA((4,))],
+        compiler_params=pltpu.CompilerParams(vmem_limit_bytes=12 * 2**20),
         name="mix",
     )(tokens, att, ow, gain)
 

time: 70.8 us -> 67.2 us (0.949)
  Pallas kernels: 69.8 us -> 66.2 us
    pallas_call x1, Pallas kernels: 5.8 us -> 3.15 us  [mix(): pl.pallas_call(mix_kernel, out_shape=(jax.ShapeDtypeStruct((TH, TW, D), B...]
    pallas_call x1, Pallas kernels: 64 us -> 63.1 us  [encode(): pl.pallas_call(encode_kernel, out_shape=(pltpu.VMEM((TH, TW, D), BF), plt...]
where the time goes in v3:
time: 67.2 us; the launch traced here: 67 us
  Pallas kernels  66.2 us (99%)
  between operations  0.83 us (1%)
    pallas_call x1, Pallas kernels, encode(): pl.pallas_call(encode_kernel, out_shape=(pltpu.VMEM((TH, TW, D), BF), plt...  63.1 us
    pallas_call x1, Pallas kernels, mix(): pl.pallas_call(mix_kernel, out_shape=(jax.ShapeDtypeStruct((TH, TW, D), B...  3.15 us

profile of v3, /device:TPU:1, one launch (start us, length us, event | category | flops | bytes accessed | tf_op | source)
XLA Modules:
  0.0 67.0 jit_solution(13636329286584791001)
XLA Ops:
  0.6 0.0 copy-start.1
  0.6 0.0 copy-start
  0.7 63.1 %encode.1 = (bf16[16,256,512]{2,1,0:T(8,128)(2,1)S(1)}, bf16[512,512]{1,0:T(8,128)(2,1)S(1)}) custom-call(bf16[69,32,512]{2,1,0:T(8,128)(2,1)} %field_hbm.1, bf16[1104,512]{1,0:T(8,128)(2,1)} %sw_hbm.1, bf16[512,1024]{1,0:T(8,128)(2,1)} %kvw_hbm.1, f32[512,512]{1,0:T(8,128)} %latents_hbm.1, bf16[512,512]{1,0:T(8,128)(2,1)} %qw_hbm.1, f32[1,512]{1,0:T(1,128)} %bitcast.5, ...), custom_call_target="tpu_custom_call" | custom-call | tf_op jit(solution)/shard_map/encode/pallas_call | solution.py:344
  63.7 0.0 copy-done.1
  63.7 0.0 copy-done
  63.7 3.1 %mix.1 = (bf16[16,256,512]{2,1,0:T(8,128)(2,1)}, f32[512,512]{1,0:T(8,128)}) custom-call(bf16[16,256,512]{2,1,0:T(8,128)(2,1)S(1)} %get-tuple-element.4.tok_in, bf16[512,512]{1,0:T(8,128)(2,1)S(1)} %get-tuple-element.5.att_ref, bf16[512,512]{1,0:T(8,128)(2,1)S(1)} %copy-done, f32[1,512]{1,0:T(1,128)S(1)} %bitcast.4), custom_call_target="tpu_custom_call" | custom-call | tf_op jit(solution)/shard_map/mix/pallas_call | solution.py:403
Async XLA Ops:
  0.6 63.1 %copy-start.1 = (f32[512]{0:T(512)S(1)}, f32[512]{0:T(512)}, u32[]{:S(2)}) copy-start(f32[512]{0:T(512)} %param.21) | copy-start | bytes 6148
  0.6 63.1 %copy-start = (bf16[512,512]{1,0:T(8,128)(2,1)S(1)}, bf16[512,512]{1,0:T(8,128)(2,1)}, u32[]{:S(2)}) copy-start(bf16[512,512]{1,0:T(8,128)(2,1)} %ow_ref.1) | copy-start | bytes 1572868

commit v4 on v3

--- a/solution.py
+++ b/solution.py
@@ -58,8 +58,7 @@
             (field_hbm, field_ref), (sw_hbm, sw_ref), (kvw_hbm, kvw_ref), (latents_hbm, latents_ref), (qw_hbm, qw_ref),
         ])
     ]
-    for load in loads:
-        load.start()
+    loads[0].start()
     lon_peer = lambda s: (lat, lax.rem(lon + s, NLOND))
     lat_peer = lambda s: (lax.rem(lat + s, NLATD), lon)
     barrier = pltpu.get_barrier_semaphore()
@@ -73,6 +72,8 @@
     wanted = jnp.where(place < 128, 2 * place, 2 * (place - 128) + 1)
     select = (source == wanted).astype(F32).astype(BF)
     loads[0].wait()
+    for load in loads[1:]:
+        load.start()
     for half in range(2):
         block = field_ref[:, :, half * 256:(half + 1) * 256].reshape(CHAN * ROWS, 256)
         both = jnp.dot(block, select, preferred_element_type=F32)

time: 67.2 us -> 67.2 us (level)
  no operation moved by 1% of the time
where the time goes in v4:
time: 67.2 us; the launch traced here: 67 us
  Pallas kernels  66.2 us (99%)
  between operations  0.83 us (1%)
    pallas_call x1, Pallas kernels, encode(): pl.pallas_call(encode_kernel, out_shape=(pltpu.VMEM((TH, TW, D), BF), plt...  63.1 us
    pallas_call x1, Pallas kernels, mix(): pl.pallas_call(mix_kernel, out_shape=(jax.ShapeDtypeStruct((TH, TW, D), B...  3.15 us

profile of v4, /device:TPU:1, one launch (start us, length us, event | category | flops | bytes accessed | tf_op | source)
XLA Modules:
  0.0 67.0 jit_solution(13880362057932439824)
XLA Ops:
  0.6 0.0 copy-start.1
  0.6 0.0 copy-start
  0.7 63.1 %encode.1 = (bf16[16,256,512]{2,1,0:T(8,128)(2,1)S(1)}, bf16[512,512]{1,0:T(8,128)(2,1)S(1)}) custom-call(bf16[69,32,512]{2,1,0:T(8,128)(2,1)} %field_hbm.1, bf16[1104,512]{1,0:T(8,128)(2,1)} %sw_hbm.1, bf16[512,1024]{1,0:T(8,128)(2,1)} %kvw_hbm.1, f32[512,512]{1,0:T(8,128)} %latents_hbm.1, bf16[512,512]{1,0:T(8,128)(2,1)} %qw_hbm.1, f32[1,512]{1,0:T(1,128)} %bitcast.5, ...), custom_call_target="tpu_custom_call" | custom-call | tf_op jit(solution)/shard_map/encode/pallas_call | solution.py:345
  63.7 0.0 copy-done.1
  63.7 0.0 copy-done
  63.7 3.1 %mix.1 = (bf16[16,256,512]{2,1,0:T(8,128)(2,1)}, f32[512,512]{1,0:T(8,128)}) custom-call(bf16[16,256,512]{2,1,0:T(8,128)(2,1)S(1)} %get-tuple-element.4.tok_in, bf16[512,512]{1,0:T(8,128)(2,1)S(1)} %get-tuple-element.5.att_ref, bf16[512,512]{1,0:T(8,128)(2,1)S(1)} %copy-done, f32[1,512]{1,0:T(1,128)S(1)} %bitcast.4), custom_call_target="tpu_custom_call" | custom-call | tf_op jit(solution)/shard_map/mix/pallas_call | solution.py:404
Async XLA Ops:
  0.6 63.1 %copy-start.1 = (f32[512]{0:T(512)S(1)}, f32[512]{0:T(512)}, u32[]{:S(2)}) copy-start(f32[512]{0:T(512)} %param.21) | copy-start | bytes 6148
  0.6 63.1 %copy-start = (bf16[512,512]{1,0:T(8,128)(2,1)S(1)}, bf16[512,512]{1,0:T(8,128)(2,1)}, u32[]{:S(2)}) copy-start(bf16[512,512]{1,0:T(8,128)(2,1)} %ow_ref.1) | copy-start | bytes 1572868
